TPU v7x, 32 devices: a whole 2x2x4 slice. The times are simulated.
32 devices in a mesh: replica: 4 (over y, x), mp: 8 (over z, core).
Axes of the slice: x: 2, y: 2, z: 4, core: 2. Of those that a mesh axis runs over, the one named last changes fastest.
Arguments:
- row_table: float32 [16384, 128], P('mp'), may hold values from -3 to 3
- grad_history: float32 [16384, 128], P('mp'), may hold values from 0.1 to 1
- touched: int32 [4, 8, 8, 256], P('replica', 'mp'), may hold values from 0 to 2047
- lookup_slot: int32 [4, 256, 32, 2], P('replica', None, 'mp'), may hold values from 0 to 2047, as said below
- pool_counts: int32 [4, 256, 32], P('replica', None, 'mp'), may hold values from 1 to 2
- cross_down: bfloat16 [4096, 512], P('mp'), may hold values from -0.09375 to 0.09375
- cross_up: bfloat16 [4096, 512], P('mp'), may hold values from -0.25 to 0.25
- cross_bias: float32 [4096], P('mp'), may hold values from -3 to 3
- cotangent: bfloat16 [4, 256, 4096], P('replica', None, 'mp'), may hold values from -0.59765625 to 0.59765625
Outputs:
- crossed: bfloat16 [4, 256, 4096], P('replica', None, 'mp')
- new_table: float32 [16384, 128], P('mp')
- fresh_history_sums: float32 [16384, 128], P('mp')
Inputs may be any that keep to these rules, and one draw needn't show every extreme that they name: For each group and each mp index m, the entries of lookup_slot over all 256 samples, the 4 features held by m and all 2 lookups are a permutation of 0 to 2047, so every owner receives exactly 256 slots from every mp index.
All inputs are finite; a program needn't handle non-finite values.
Results may differ from a plain program's by a relative error of at most 0.017.
Values may be sent and summed in bfloat16 or wider, within the bound.
A program may use at most 64 MiB of HBM per device.

v0:
```python
import functools

import jax
import jax.numpy as jnp
from jax import lax
from jax.experimental import pallas as pl
from jax.experimental.pallas import tpu as pltpu
from jax.sharding import PartitionSpec as P

learn_rate = 0.5
epsilon = 1e-06
LANES = 128
bf16 = jnp.bfloat16
f32 = jnp.float32


def flip(index, distance, count):
    result = 0
    bit = 1
    while bit < count:
        result = result + bit * lax.rem(
            lax.div(jnp.int32(index), jnp.int32(bit)) + lax.div(jnp.int32(distance), jnp.int32(bit)),
            jnp.int32(2),
        )
        bit *= 2
    return result


def steps(order, body):
    if len(order) <= 8:
        for d in order:
            body(d)
    else:
        first, stride = order[0], order[1] - order[0]
        lax.fori_loop(0, len(order), lambda i, c: (body(first + stride * i), c)[1], 0)


def ones_where(mask):
    return jnp.where(mask, 1.0, 0.0).astype(bf16)


def kernel(
    n,
    nr,
    table_ref,
    wanted_ref,
    slots_ref,
    counts_ref,
    down_ref,
    up_ref,
    bias_ref,
    cot_ref,
    crossed_ref,
    grad_ref,
    table_half,
    onehot,
    rows_out,
    rows_in,
    columns,
    divisors,
    pick,
    place,
    owned,
    pool_sum,
    pooled_half,
    weighted,
    mate_out,
    mate_in,
    own,
    pair_out,
    pair_in,
    full,
    grad_half,
    grads_out,
    grads_in,
    row_sum,
    row_part,
    row_part_in,
    row_reduced,
    row_full,
    rows_send,
    rows_recv,
    grads_send,
    grads_recv,
    mate_send,
    mate_recv,
    pair_send,
    pair_recv,
    full_send,
    full_recv,
    pass_send,
    pass_recv,
    row_part_send,
    row_part_recv,
    row_full_send,
    row_full_recv,
):
    me = lax.axis_index("mp")
    group = lax.axis_index("replica")
    cap = wanted_ref.shape[1]
    rows, width = table_ref.shape
    features, hot, samples = slots_ref.shape
    rank = down_ref.shape[1]
    piece = min(cap, LANES)
    near = list(range(1, n))
    far = near[::-1]
    group_far = list(range(nr - 1, 0, -1))

    barrier = pltpu.get_barrier_semaphore()
    for_mp = lambda d: pl.semaphore_signal(
        barrier, inc=1, device_id={"mp": flip(me, d, n)}, device_id_type=pl.DeviceIdType.MESH
    )
    for_replica = lambda e: pl.semaphore_signal(
        barrier, inc=1, device_id={"replica": flip(group, e, nr)}, device_id_type=pl.DeviceIdType.MESH
    )
    steps(far, for_mp)
    steps(group_far, for_replica)

    def to_mp(src, dst, send, recv, d):
        return pltpu.make_async_remote_copy(
            src_ref=src,
            dst_ref=dst,
            send_sem=send.at[d],
            recv_sem=recv.at[d],
            device_id={"mp": flip(me, d, n)},
            device_id_type=pl.DeviceIdType.MESH,
        )

    def to_replica(src, dst, send, recv, e):
        return pltpu.make_async_remote_copy(
            src_ref=src,
            dst_ref=dst,
            send_sem=send.at[e],
            recv_sem=recv.at[e],
            device_id={"replica": flip(group, e, nr)},
            device_id_type=pl.DeviceIdType.MESH,
        )

    rows_copy = lambda d: to_mp(rows_out.at[d], rows_in.at[d], rows_send, rows_recv, d)
    grads_copy = lambda d: to_mp(grads_out.at[d], grads_in.at[d], grads_send, grads_recv, d)
    row_part_copy = lambda e: to_replica(
        row_part.at[flip(group, e, nr)], row_part_in.at[e], row_part_send, row_part_recv, e
    )
    row_full_copy = lambda e: to_replica(
        row_reduced, row_full.at[group], row_full_send, row_full_recv, e
    )

    pairs = n // 2
    half = lax.rem(me, jnp.int32(2))
    pair = lax.div(me, jnp.int32(2))
    mate = me + 1 - 2 * half
    pair_near = list(range(1, pairs))
    pair_far = pair_near[::-1]

    def to_device(src, dst, send, recv, device):
        return pltpu.make_async_remote_copy(
            src_ref=src,
            dst_ref=dst,
            send_sem=send,
            recv_sem=recv,
            device_id={"mp": device},
            device_id_type=pl.DeviceIdType.MESH,
        )

    across = lambda e: flip(pair, e, pairs)
    mate_copy = lambda e: to_device(
        mate_out.at[across(e)], mate_in.at[e], mate_send.at[e], mate_recv.at[e], mate
    )
    pair_copy = lambda e: to_device(
        pair_out.at[e], pair_in.at[e], pair_send.at[e], pair_recv.at[e], 2 * across(e) + half
    )
    full_copy = lambda e: to_device(
        full.at[half, pair],
        full.at[half, pair],
        full_send.at[e],
        full_recv.at[e],
        2 * across(e) + half,
    )
    pass_copy = lambda h, e: to_device(
        full.at[h, across(e)], full.at[h, across(e)], pass_send.at[e], pass_recv.at[e], mate
    )

    table_half[...] = table_ref[...].astype(bf16)
    lane = lax.broadcasted_iota(jnp.int32, (cap, LANES), 1)

    def gather(d):
        row = wanted_ref[pl.ds(flip(me, d, n), 1), :]
        column = jnp.broadcast_to(row, (LANES, cap)).T
        for j in range(rows // LANES):
            onehot[:, j * LANES : (j + 1) * LANES] = ones_where(column == lane + j * LANES)
        return jnp.dot(onehot[...], table_half[...], preferred_element_type=f32).astype(bf16)

    rows_out[n - 1] = gather(n - 1)
    pl.semaphore_wait(barrier, n - 1 + nr - 1)
    rows_copy(n - 1).start()

    def send_rows(d):
        rows_out[d] = gather(d)
        rows_copy(d).start()

    steps(far[1:], send_rows)
    rows_in[0] = gather(0)

    slot_rows = {}
    for f in range(features):
        count = counts_ref[f : f + 1, :]
        divisors[f] = jnp.broadcast_to(count.astype(f32), (width, samples)).T
        for k in range(hot):
            row = jnp.where(k < count, slots_ref[f, k : k + 1, :], -1)
            slot_rows[f, k] = row
            columns[k * features + f] = jnp.broadcast_to(row, (LANES, samples)).T
    piece_lane = lax.broadcasted_iota(jnp.int32, (samples, piece), 1)
    cap_row = lax.broadcasted_iota(jnp.int32, (cap, samples), 0)
    block_row = lax.broadcasted_iota(jnp.int32, (LANES, cap), 0)

    def build_pick(d):
        base = flip(me, d, n) * cap
        for f in range(features):
            for j in range(cap // piece):
                mask = None
                for k in range(hot):
                    hit = columns[k * features + f][:, :piece] - (base + j * piece) == piece_lane
                    mask = hit if mask is None else mask | hit
                pick[d, f * samples : (f + 1) * samples, j * piece : (j + 1) * piece] = ones_where(mask)

    def build_place(d):
        base = flip(me, d, n) * cap
        for f in range(features):
            mask = None
            for k in range(hot):
                hit = slot_rows[f, k] - base == cap_row
                mask = hit if mask is None else mask | hit
            place[d, :, f * samples : (f + 1) * samples] = ones_where(mask)

    def build_owned(d):
        row = wanted_ref[pl.ds(flip(me, d, n), 1), :]
        for j in range(rows // LANES):
            owned[d, j * LANES : (j + 1) * LANES, :] = ones_where(row == block_row + j * LANES)

    steps([0] + near, build_pick)
    pool_sum[...] = jnp.dot(pick[0], rows_in[0], preferred_element_type=f32)
    steps([0] + near, build_place)
    steps([0] + near, build_owned)

    def pool(d):
        rows_copy(d).wait_recv()
        pool_sum[...] += jnp.dot(pick[d], rows_in[d], preferred_element_type=f32)

    steps(near, pool)

    rows_half = samples // 2
    for f in range(features):
        cut = slice(f * width, (f + 1) * width)
        value = (pool_sum[f * samples : (f + 1) * samples, :] / divisors[f]).astype(bf16)
        change = (cot_ref[:, cut].astype(f32) * value.astype(f32)).astype(bf16)
        for h in range(2):
            pooled_half[h, :, cut] = value[h * rows_half : (h + 1) * rows_half]
            weighted[h, :, cut] = change[h * rows_half : (h + 1) * rows_half]

    def partial(h):
        low = jnp.dot(pooled_half[h], down_ref[...], preferred_element_type=f32)
        back = jnp.dot(weighted[h], up_ref[...], preferred_element_type=f32)
        return low.reshape(pairs, -1, rank), back.reshape(pairs, -1, rank)

    low, back = partial(1 - half)
    mate_out[:, :, :rank] = low.astype(bf16)
    mate_out[:, :, rank:] = back.astype(bf16)
    steps(pair_far + [0], lambda e: mate_copy(e).start())
    low, back = partial(half)
    own[:, :, :rank] = low
    own[:, :, rank:] = back

    def send_pair(e):
        mate_copy(e).wait_recv()
        pair_out[e] = (own[across(e)] + mate_in[e].astype(f32)).astype(bf16)
        pair_copy(e).start()

    steps(pair_far, send_pair)
    mate_copy(0).wait_recv()
    own[pair] = own[pair] + mate_in[0].astype(f32)

    def add_pair(e):
        pair_copy(e).wait_recv()
        own[pair] = own[pair] + pair_in[e].astype(f32)

    steps(pair_near, add_pair)
    full[half, pair] = own[pair].astype(bf16)
    steps(pair_far, lambda e: full_copy(e).start())
    pass_copy(half, 0).start()

    def pass_on(e):
        full_copy(e).wait_recv()
        pass_copy(half, e).start()

    steps(pair_near, pass_on)
    steps([0] + pair_near, lambda e: pass_copy(1 - half, e).wait_recv())

    low_half = full[:, :, :, :rank].reshape(samples, rank)
    back_half = full[:, :, :, rank:].reshape(samples, rank)
    transposed = (((1,), (1,)), ((), ()))
    for f in range(features):
        cut = slice(f * width, (f + 1) * width)
        scaled = (
            lax.dot_general(low_half, up_ref[cut, :], transposed, preferred_element_type=f32)
            + bias_ref[:, cut]
        )
        wide = pooled_half[:, :, cut].reshape(samples, width).astype(f32)
        crossed_ref[:, cut] = (wide * scaled + wide).astype(bf16)
        upstream = cot_ref[:, cut].astype(f32)
        pool_grad = (
            upstream * scaled
            + upstream
            + lax.dot_general(back_half, down_ref[cut, :], transposed, preferred_element_type=f32)
        )
        grad_half[f * samples : (f + 1) * samples, :] = (pool_grad / divisors[f]).astype(bf16)

    def send_grads(d):
        grads_out[d] = jnp.dot(place[d], grad_half[...], preferred_element_type=f32).astype(bf16)
        grads_copy(d).start()

    steps(far, send_grads)
    grads_in[0] = jnp.dot(place[0], grad_half[...], preferred_element_type=f32).astype(bf16)
    row_sum[...] = jnp.dot(owned[0], grads_in[0], preferred_element_type=f32)

    def collect(d):
        grads_copy(d).wait_recv()
        row_sum[...] += jnp.dot(owned[d], grads_in[d], preferred_element_type=f32)

    steps(near, collect)

    row_part[...] = row_sum[...].reshape(row_part.shape).astype(bf16)
    steps(group_far, lambda e: row_part_copy(e).start())
    total = row_part[group].astype(f32)
    if nr <= 8:
        for e in group_far[::-1]:
            row_part_copy(e).wait_recv()
            total = total + row_part_in[e].astype(f32)
    else:

        def add_rows(i, value):
            row_part_copy(i + 1).wait_recv()
            return value + row_part_in[i + 1].astype(f32)

        total = lax.fori_loop(0, nr - 1, add_rows, total)
    row_reduced[...] = total.astype(bf16)
    steps(group_far, lambda e: row_full_copy(e).start())
    row_full[group] = row_reduced[...]
    steps(group_far[::-1], lambda e: row_full_copy(e).wait_recv())
    grad_ref[...] = row_full[...].reshape(rows, width)

    steps(near, lambda d: rows_copy(d).wait_send())
    steps([0] + pair_near, lambda e: mate_copy(e).wait_send())
    steps(pair_near, lambda e: pair_copy(e).wait_send())
    steps(pair_near, lambda e: full_copy(e).wait_send())
    steps([0] + pair_near, lambda e: pass_copy(half, e).wait_send())
    steps(near, lambda d: grads_copy(d).wait_send())
    steps(group_far, lambda e: row_part_copy(e).wait_send())
    steps(group_far, lambda e: row_full_copy(e).wait_send())


def shards(
    n,
    nr,
    row_table,
    grad_history,
    touched,
    lookup_slot,
    pool_counts,
    cross_down,
    cross_up,
    cross_bias,
    cotangent,
):
    rows, width = row_table.shape
    wanted = touched[0, 0]
    cap = wanted.shape[1]
    counts = pool_counts[0].T
    slots = lookup_slot[0].transpose(1, 2, 0)
    features, hot, samples = slots.shape
    rank = cross_down.shape[1]
    dma = pltpu.SemaphoreType.DMA
    vmem = pl.BlockSpec(memory_space=pltpu.VMEM)
    lookups = features * samples
    pieces = (n // 2, samples // n, 2 * rank)
    crossed, summed = pl.pallas_call(
        functools.partial(kernel, n, nr),
        out_shape=(
            jax.ShapeDtypeStruct((samples, features * width), bf16),
            jax.ShapeDtypeStruct((rows, width), bf16),
        ),
        in_specs=[vmem] * 8,
        out_specs=(vmem, vmem),
        scratch_shapes=[
            pltpu.VMEM((rows, width), bf16),
            pltpu.VMEM((cap, rows), bf16),
            pltpu.VMEM((n, cap, width), bf16),
            pltpu.VMEM((n, cap, width), bf16),
            pltpu.VMEM((hot * features, samples, LANES), jnp.int32),
            pltpu.VMEM((features, samples, width), f32),
            pltpu.VMEM((n, lookups, cap), bf16),
            pltpu.VMEM((n, cap, lookups), bf16),
            pltpu.VMEM((n, rows, cap), bf16),
            pltpu.VMEM((lookups, width), f32),
            pltpu.VMEM((2, samples // 2, features * width), bf16),
            pltpu.VMEM((2, samples // 2, features * width), bf16),
            pltpu.VMEM(pieces, bf16),
            pltpu.VMEM(pieces, bf16),
            pltpu.VMEM(pieces, f32),
            pltpu.VMEM(pieces, bf16),
            pltpu.VMEM(pieces, bf16),
            pltpu.VMEM((2, *pieces), bf16),
            pltpu.VMEM((lookups, width), bf16),
            pltpu.VMEM((n, cap, width), bf16),
            pltpu.VMEM((n, cap, width), bf16),
            pltpu.VMEM((rows, width), f32),
            pltpu.VMEM((nr, rows // nr, width), bf16),
            pltpu.VMEM((nr, rows // nr, width), bf16),
            pltpu.VMEM((rows // nr, width), bf16),
            pltpu.VMEM((nr, rows // nr, width), bf16),
        ]
        + [dma((n,))] * 4
        + [dma((n // 2,))] * 8
        + [dma((nr,))] * 4,
        compiler_params=pltpu.CompilerParams(
            collective_id=0, has_side_effects=True, vmem_limit_bytes=56 * 1024 * 1024
        ),
        cost_estimate=pl.CostEstimate(flops=10**9 * 6, bytes_accessed=10**7, transcendentals=0),
    )(row_table, wanted, slots, counts, cross_down, cross_up, cross_bias[None, :], cotangent[0])
    summed = summed.astype(f32)
    fresh_history_sums = grad_history + summed * summed
    new_table = row_table - learn_rate * summed / (jnp.sqrt(fresh_history_sums) + epsilon)
    return (crossed[None], new_table, fresh_history_sums)


def solution(mesh):
    in_specs = (
        P("mp", None),
        P("mp", None),
        P("replica", "mp", None, None),
        P("replica", None, "mp", None),
        P("replica", None, "mp"),
        P("mp", None),
        P("mp", None),
        P("mp"),
        P("replica", None, "mp"),
    )
    out_specs = (P("replica", None, "mp"), P("mp", None), P("mp", None))
    body = functools.partial(shards, mesh.shape["mp"], mesh.shape["replica"])
    return jax.shard_map(body, mesh=mesh, in_specs=in_specs, out_specs=out_specs, check_vma=False)
```

profile of v0, /device:TPU:0, one launch (start us, length us, event | category | flops | bytes accessed | tf_op | source)
XLA Modules:
  0.0 75.7 jit_solution(15188645073667129075)
XLA Ops:
  0.6 0.0 copy-start
  0.6 0.0 copy-start.1
  0.7 71.4 %shard_map.112 = (bf16[256,512]{1,0:T(8,128)(2,1)}, bf16[2048,128]{1,0:T(8,128)(2,1)}) custom-call(f32[2048,128]{1,0:T(8,128)} %table_ref.1, s32[8,256]{1,0:T(8,128)} %bitcast.12, s32[4,2,256]{2,1,0:T(2,128)} %bitcast.13, s32[4,256]{1,0:T(4,128)} %bitcast.14, bf16[512,512]{1,0:T(8,128)(2,1)} %down_ref.1, bf16[512,512]{1,0:T(8,128)(2,1)} %up_ref.1, ...), custom_call_target="tpu_custom_call" | custom-call | flops 6000000000 | bytes 10000000 | tf_op jit(solution)/shard_map/pallas_call | solution.py:385
  72.0 0.0 copy-done
  72.1 0.0 copy-done.1
  72.1 0.0 copy-start.2
  72.1 2.9 %fusion.1 = (f32[2048,128]{1,0:T(8,128)}, f32[2048,128]{1,0:T(8,128)}) fusion(f32[2048,128]{1,0:T(8,128)S(1)} %copy-done, bf16[2048,128]{1,0:T(8,128)(2,1)} %get-tuple-element.6, f32[2048,128]{1,0:T(8,128)S(1)} %copy-done.1), kind=kLoop, calls=%fused_computation.3 | loop fusion | flops 1835008 | bytes 4718592 | tf_op jit(solution)/shard_map/sub | solution.py:431
  75.0 0.0 copy-done.2
  75.0 0.7 copy.13
Async XLA Ops:
  0.6 71.4 %copy-start = (f32[2048,128]{1,0:T(8,128)S(1)}, f32[2048,128]{1,0:T(8,128)}, u32[]{:S(2)}) copy-start(f32[2048,128]{1,0:T(8,128)} %table_ref.1) | copy-start | bytes 3145732
  0.6 71.4 %copy-start.1 = (f32[2048,128]{1,0:T(8,128)S(1)}, f32[2048,128]{1,0:T(8,128)}, u32[]{:S(2)}) copy-start(f32[2048,128]{1,0:T(8,128)} %param.10) | copy-start | bytes 3145732
  72.1 2.9 %copy-start.2 = (bf16[256,512]{1,0:T(8,128)(2,1)S(1)}, bf16[256,512]{1,0:T(8,128)(2,1)}, u32[]{:S(2)}) copy-start(bf16[256,512]{1,0:T(8,128)(2,1)} %get-tuple-element.5) | copy-start | bytes 786436
where the time goes:
time: 75.8 us; the launch traced here: 75.7 us
  Pallas kernels  71.4 us (94%)
  other arithmetic  2.9 us (4%)
    pallas_call x1, Pallas kernels, shards(): pl.pallas_call(functools.partial(kernel, n, nr), out_shape=(jax.ShapeDtyp...  71.4 us
    sub x1, other arithmetic, shards(): row_table - learn_rate * summed / (jnp.sqrt(fresh_history_sums) + epsilon)  2.9 us

commit v1 on v0

--- a/solution.py
+++ b/solution.py
@@ -76,7 +76,7 @@
     row_sum,
     row_part,
     row_part_in,
-    row_reduced,
+    row_total,
     row_full,
     rows_send,
     rows_recv,
@@ -137,12 +137,18 @@
         )
 
     rows_copy = lambda d: to_mp(rows_out.at[d], rows_in.at[d], rows_send, rows_recv, d)
-    grads_copy = lambda d: to_mp(grads_out.at[d], grads_in.at[d], grads_send, grads_recv, d)
-    row_part_copy = lambda e: to_replica(
-        row_part.at[flip(group, e, nr)], row_part_in.at[e], row_part_send, row_part_recv, e
-    )
-    row_full_copy = lambda e: to_replica(
-        row_reduced, row_full.at[group], row_full_send, row_full_recv, e
+    grads_copy = lambda h, d: to_mp(
+        grads_out.at[h, d], grads_in.at[h, d], grads_send.at[h], grads_recv.at[h], d
+    )
+    row_part_copy = lambda h, e: to_replica(
+        row_part.at[h, flip(group, e, nr)],
+        row_part_in.at[h, e],
+        row_part_send.at[h],
+        row_part_recv.at[h],
+        e,
+    )
+    row_full_copy = lambda h, e: to_replica(
+        row_full.at[h, group], row_full.at[h, group], row_full_send.at[h], row_full_recv.at[h], e
     )
 
     pairs = n // 2
@@ -239,8 +245,6 @@
 
     steps([0] + near, build_pick)
     pool_sum[...] = jnp.dot(pick[0], rows_in[0], preferred_element_type=f32)
-    steps([0] + near, build_place)
-    steps([0] + near, build_owned)
 
     def pool(d):
         rows_copy(d).wait_recv()
@@ -276,6 +280,7 @@
         pair_copy(e).start()
 
     steps(pair_far, send_pair)
+    steps([0] + near, build_place)
     mate_copy(0).wait_recv()
     own[pair] = own[pair] + mate_in[0].astype(f32)
 
@@ -298,6 +303,8 @@
     low_half = full[:, :, :, :rank].reshape(samples, rank)
     back_half = full[:, :, :, rank:].reshape(samples, rank)
     transposed = (((1,), (1,)), ((), ()))
+    left = lax.broadcasted_iota(jnp.int32, (samples, width), 1) < width // 2
+    swap = lambda value: pltpu.roll(value, width // 2, 1)
     for f in range(features):
         cut = slice(f * width, (f + 1) * width)
         scaled = (
@@ -312,50 +319,94 @@
             + upstream
             + lax.dot_general(back_half, down_ref[cut, :], transposed, preferred_element_type=f32)
         )
-        grad_half[f * samples : (f + 1) * samples, :] = (pool_grad / divisors[f]).astype(bf16)
-
-    def send_grads(d):
-        grads_out[d] = jnp.dot(place[d], grad_half[...], preferred_element_type=f32).astype(bf16)
-        grads_copy(d).start()
-
-    steps(far, send_grads)
-    grads_in[0] = jnp.dot(place[0], grad_half[...], preferred_element_type=f32).astype(bf16)
-    row_sum[...] = jnp.dot(owned[0], grads_in[0], preferred_element_type=f32)
-
-    def collect(d):
-        grads_copy(d).wait_recv()
-        row_sum[...] += jnp.dot(owned[d], grads_in[d], preferred_element_type=f32)
-
-    steps(near, collect)
-
-    row_part[...] = row_sum[...].reshape(row_part.shape).astype(bf16)
-    steps(group_far, lambda e: row_part_copy(e).start())
-    total = row_part[group].astype(f32)
-    if nr <= 8:
-        for e in group_far[::-1]:
-            row_part_copy(e).wait_recv()
-            total = total + row_part_in[e].astype(f32)
-    else:
-
-        def add_rows(i, value):
-            row_part_copy(i + 1).wait_recv()
-            return value + row_part_in[i + 1].astype(f32)
-
-        total = lax.fori_loop(0, nr - 1, add_rows, total)
-    row_reduced[...] = total.astype(bf16)
-    steps(group_far, lambda e: row_full_copy(e).start())
-    row_full[group] = row_reduced[...]
-    steps(group_far[::-1], lambda e: row_full_copy(e).wait_recv())
-    grad_ref[...] = row_full[...].reshape(rows, width)
+        value = (pool_grad / divisors[f]).astype(bf16).astype(f32)
+        low_lanes = jnp.where(left, value, 0.0)
+        high_lanes = jnp.where(left, 0.0, value)
+        span = slice(f * samples, (f + 1) * samples)
+        grad_half[0, 0, span, :] = low_lanes.astype(bf16)
+        grad_half[0, 1, span, :] = swap(low_lanes).astype(bf16)
+        grad_half[1, 0, span, :] = swap(high_lanes).astype(bf16)
+        grad_half[1, 1, span, :] = high_lanes.astype(bf16)
+
+    def packed_grads(h, d):
+        return (
+            jnp.dot(place[d, : cap // 2], grad_half[h, 0], preferred_element_type=f32)
+            + jnp.dot(place[d, cap // 2 :], grad_half[h, 1], preferred_element_type=f32)
+        ).astype(bf16)
+
+    for h in range(2):
+
+        def send_grads(d):
+            grads_out[h, d] = packed_grads(h, d)
+            grads_copy(h, d).start()
+
+        steps(far, send_grads)
+    for h in range(2):
+        grads_in[h, 0] = packed_grads(h, 0)
+    steps([0] + near, build_owned)
+
+    def collect(h, d):
+        value = grads_in[h, d].astype(f32)
+        other = swap(value)
+        first, second = (value, other) if h == 0 else (other, value)
+        slots = jnp.concatenate([first, second], axis=0).astype(bf16)
+        return jnp.dot(owned[d], slots, preferred_element_type=f32)
+
+    share = rows // nr
+    row_left = lax.broadcasted_iota(jnp.int32, (share // 2, width), 1) < width // 2
+
+    def gather_half(h):
+        row_sum[...] = collect(h, 0)
+
+        def arrive(d):
+            grads_copy(h, d).wait_recv()
+            row_sum[...] += collect(h, d)
+
+        steps(near, arrive)
+        for q in range(nr):
+            top = row_sum[q * share : q * share + share // 2, :]
+            bottom = row_sum[q * share + share // 2 : (q + 1) * share, :]
+            if h == 0:
+                packed = jnp.where(row_left, top, swap(bottom))
+            else:
+                packed = jnp.where(row_left, swap(top), bottom)
+            row_part[h, q] = packed.astype(bf16)
+        steps(group_far, lambda e: row_part_copy(h, e).start())
+
+    def reduce_half(h):
+        row_total[...] = row_part[h, group].astype(f32)
+
+        def arrive(e):
+            row_part_copy(h, e).wait_recv()
+            row_total[...] += row_part_in[h, e].astype(f32)
+
+        steps(group_far[::-1], arrive)
+        row_full[h, group] = row_total[...].astype(bf16)
+        steps(group_far, lambda e: row_full_copy(h, e).start())
+
+    gather_half(0)
+    reduce_half(0)
+    gather_half(1)
+    reduce_half(1)
+    for h in range(2):
+        steps(group_far[::-1], lambda e: row_full_copy(h, e).wait_recv())
+    for q in range(nr):
+        first = row_full[0, q].astype(f32)
+        second = row_full[1, q].astype(f32)
+        top = jnp.where(row_left, first, swap(second))
+        bottom = jnp.where(row_left, swap(first), second)
+        grad_ref[q * share : q * share + share // 2, :] = top.astype(bf16)
+        grad_ref[q * share + share // 2 : (q + 1) * share, :] = bottom.astype(bf16)
 
     steps(near, lambda d: rows_copy(d).wait_send())
     steps([0] + pair_near, lambda e: mate_copy(e).wait_send())
     steps(pair_near, lambda e: pair_copy(e).wait_send())
     steps(pair_near, lambda e: full_copy(e).wait_send())
     steps([0] + pair_near, lambda e: pass_copy(half, e).wait_send())
-    steps(near, lambda d: grads_copy(d).wait_send())
-    steps(group_far, lambda e: row_part_copy(e).wait_send())
-    steps(group_far, lambda e: row_full_copy(e).wait_send())
+    for h in range(2):
+        steps(near, lambda d: grads_copy(h, d).wait_send())
+        steps(group_far, lambda e: row_part_copy(h, e).wait_send())
+        steps(group_far, lambda e: row_full_copy(h, e).wait_send())
 
 
 def shards(
@@ -409,18 +460,19 @@
             pltpu.VMEM(pieces, bf16),
             pltpu.VMEM(pieces, bf16),
             pltpu.VMEM((2, *pieces), bf16),
-            pltpu.VMEM((lookups, width), bf16),
-            pltpu.VMEM((n, cap, width), bf16),
-            pltpu.VMEM((n, cap, width), bf16),
+            pltpu.VMEM((2, 2, lookups, width), bf16),
+            pltpu.VMEM((2, n, cap // 2, width), bf16),
+            pltpu.VMEM((2, n, cap // 2, width), bf16),
             pltpu.VMEM((rows, width), f32),
-            pltpu.VMEM((nr, rows // nr, width), bf16),
-            pltpu.VMEM((nr, rows // nr, width), bf16),
-            pltpu.VMEM((rows // nr, width), bf16),
-            pltpu.VMEM((nr, rows // nr, width), bf16),
+            pltpu.VMEM((2, nr, rows // nr // 2, width), bf16),
+            pltpu.VMEM((2, nr, rows // nr // 2, width), bf16),
+            pltpu.VMEM((rows // nr // 2, width), f32),
+            pltpu.VMEM((2, nr, rows // nr // 2, width), bf16),
         ]
-        + [dma((n,))] * 4
+        + [dma((n,))] * 2
+        + [dma((2, n))] * 2
         + [dma((n // 2,))] * 8
-        + [dma((nr,))] * 4,
+        + [dma((2, nr))] * 4,
         compiler_params=pltpu.CompilerParams(
             collective_id=0, has_side_effects=True, vmem_limit_bytes=56 * 1024 * 1024
         ),

time: 75.8 us -> 77.5 us (1.022)
  Pallas kernels: 71.4 us -> 73.1 us
    pallas_call x1, Pallas kernels: 71.4 us -> 73.1 us  [shards(): pl.pallas_call(functools.partial(kernel, n, nr), out_shape=(jax.ShapeDtyp...]
where the time goes in v1:
time: 77.5 us; the launch traced here: 77.4 us
  Pallas kernels  73.1 us (94%)
  other arithmetic  2.9 us (4%)
    pallas_call x1, Pallas kernels, shards(): pl.pallas_call(functools.partial(kernel, n, nr), out_shape=(jax.ShapeDtyp...  73.1 us
    sub x1, other arithmetic, shards(): row_table - learn_rate * summed / (jnp.sqrt(fresh_history_sums) + epsilon)  2.9 us

profile of v1, /device:TPU:0, one launch (start us, length us, event | category | flops | bytes accessed | tf_op | source)
XLA Modules:
  0.0 77.4 jit_solution(14437629710908527150)
XLA Ops:
  0.6 0.0 copy-start
  0.6 0.0 copy-start.1
  0.7 73.1 %shard_map.112 = (bf16[256,512]{1,0:T(8,128)(2,1)}, bf16[2048,128]{1,0:T(8,128)(2,1)}) custom-call(f32[2048,128]{1,0:T(8,128)} %table_ref.1, s32[8,256]{1,0:T(8,128)} %bitcast.12, s32[4,2,256]{2,1,0:T(2,128)} %bitcast.13, s32[4,256]{1,0:T(4,128)} %bitcast.14, bf16[512,512]{1,0:T(8,128)(2,1)} %down_ref.1, bf16[512,512]{1,0:T(8,128)(2,1)} %up_ref.1, ...), custom_call_target="tpu_custom_call" | custom-call | flops 6000000000 | bytes 10000000 | tf_op jit(solution)/shard_map/pallas_call | solution.py:436
  73.7 0.0 copy-done
  73.7 0.0 copy-done.1
  73.7 0.0 copy-start.2
  73.7 2.9 %fusion.1 = (f32[2048,128]{1,0:T(8,128)}, f32[2048,128]{1,0:T(8,128)}) fusion(f32[2048,128]{1,0:T(8,128)S(1)} %copy-done, bf16[2048,128]{1,0:T(8,128)(2,1)} %get-tuple-element.6, f32[2048,128]{1,0:T(8,128)S(1)} %copy-done.1), kind=kLoop, calls=%fused_computation.3 | loop fusion | flops 1835008 | bytes 4718592 | tf_op jit(solution)/shard_map/sub | solution.py:483
  76.6 0.0 copy-done.2
  76.6 0.7 copy.13
Async XLA Ops:
  0.6 73.1 %copy-start = (f32[2048,128]{1,0:T(8,128)S(1)}, f32[2048,128]{1,0:T(8,128)}, u32[]{:S(2)}) copy-start(f32[2048,128]{1,0:T(8,128)} %table_ref.1) | copy-start | bytes 3145732
  0.6 73.1 %copy-start.1 = (f32[2048,128]{1,0:T(8,128)S(1)}, f32[2048,128]{1,0:T(8,128)}, u32[]{:S(2)}) copy-start(f32[2048,128]{1,0:T(8,128)} %param.10) | copy-start | bytes 3145732
  73.7 2.9 %copy-start.2 = (bf16[256,512]{1,0:T(8,128)(2,1)S(1)}, bf16[256,512]{1,0:T(8,128)(2,1)}, u32[]{:S(2)}) copy-start(bf16[256,512]{1,0:T(8,128)(2,1)} %get-tuple-element.5) | copy-start | bytes 786436

commit v2 on v0

--- a/solution.py
+++ b/solution.py
@@ -239,8 +239,6 @@
 
     steps([0] + near, build_pick)
     pool_sum[...] = jnp.dot(pick[0], rows_in[0], preferred_element_type=f32)
-    steps([0] + near, build_place)
-    steps([0] + near, build_owned)
 
     def pool(d):
         rows_copy(d).wait_recv()
@@ -276,6 +274,7 @@
         pair_copy(e).start()
 
     steps(pair_far, send_pair)
+    steps([0] + near, build_place)
     mate_copy(0).wait_recv()
     own[pair] = own[pair] + mate_in[0].astype(f32)
 
@@ -319,6 +318,7 @@
         grads_copy(d).start()
 
     steps(far, send_grads)
+    steps([0] + near, build_owned)
     grads_in[0] = jnp.dot(place[0], grad_half[...], preferred_element_type=f32).astype(bf16)
     row_sum[...] = jnp.dot(owned[0], grads_in[0], preferred_element_type=f32)
 

time: 75.8 us -> 75.8 us (level)
  no operation moved by 1% of the time
where the time goes in v2:
time: 75.8 us; the launch traced here: 75.7 us
  Pallas kernels  71.4 us (94%)
  other arithmetic  2.9 us (4%)
    pallas_call x1, Pallas kernels, shards(): pl.pallas_call(functools.partial(kernel, n, nr), out_shape=(jax.ShapeDtyp...  71.4 us
    sub x1, other arithmetic, shards(): row_table - learn_rate * summed / (jnp.sqrt(fresh_history_sums) + epsilon)  2.9 us

profile of v2, /device:TPU:0, one launch (start us, length us, event | category | flops | bytes accessed | tf_op | source)
XLA Modules:
  0.0 75.7 jit_solution(8066520243800502281)
XLA Ops:
  0.6 0.0 copy-start
  0.6 0.0 copy-start.1
  0.7 71.4 %shard_map.112 = (bf16[256,512]{1,0:T(8,128)(2,1)}, bf16[2048,128]{1,0:T(8,128)(2,1)}) custom-call(f32[2048,128]{1,0:T(8,128)} %table_ref.1, s32[8,256]{1,0:T(8,128)} %bitcast.12, s32[4,2,256]{2,1,0:T(2,128)} %bitcast.13, s32[4,256]{1,0:T(4,128)} %bitcast.14, bf16[512,512]{1,0:T(8,128)(2,1)} %down_ref.1, bf16[512,512]{1,0:T(8,128)(2,1)} %up_ref.1, ...), custom_call_target="tpu_custom_call" | custom-call | flops 6000000000 | bytes 10000000 | tf_op jit(solution)/shard_map/pallas_call | solution.py:385
  72.0 0.0 copy-done
  72.1 0.0 copy-done.1
  72.1 0.0 copy-start.2
  72.1 2.9 %fusion.1 = (f32[2048,128]{1,0:T(8,128)}, f32[2048,128]{1,0:T(8,128)}) fusion(f32[2048,128]{1,0:T(8,128)S(1)} %copy-done, bf16[2048,128]{1,0:T(8,128)(2,1)} %get-tuple-element.6, f32[2048,128]{1,0:T(8,128)S(1)} %copy-done.1), kind=kLoop, calls=%fused_computation.3 | loop fusion | flops 1835008 | bytes 4718592 | tf_op jit(solution)/shard_map/sub | solution.py:431
  75.0 0.0 copy-done.2
  75.0 0.7 copy.13
Async XLA Ops:
  0.6 71.4 %copy-start = (f32[2048,128]{1,0:T(8,128)S(1)}, f32[2048,128]{1,0:T(8,128)}, u32[]{:S(2)}) copy-start(f32[2048,128]{1,0:T(8,128)} %table_ref.1) | copy-start | bytes 3145732
  0.6 71.4 %copy-start.1 = (f32[2048,128]{1,0:T(8,128)S(1)}, f32[2048,128]{1,0:T(8,128)}, u32[]{:S(2)}) copy-start(f32[2048,128]{1,0:T(8,128)} %param.10) | copy-start | bytes 3145732
  72.1 2.9 %copy-start.2 = (bf16[256,512]{1,0:T(8,128)(2,1)S(1)}, bf16[256,512]{1,0:T(8,128)(2,1)}, u32[]{:S(2)}) copy-start(bf16[256,512]{1,0:T(8,128)(2,1)} %get-tuple-element.5) | copy-start | bytes 786436
